TPU v7x, 128 devices: a whole 4x4x4 slice. The times are simulated.
128 devices in a mesh: row: 8 (over x, core), col: 16 (over y, z).
Axes of the slice: x: 4, y: 4, z: 4, core: 2. Of those that a mesh axis runs over, the one named last changes fastest.
Arguments:
- hamiltonian: bfloat16 [5824, 5824], P('row', 'col'), may hold values from -6 to 6
- new_atom: int32 [448], replicated, may hold values from 0 to 447, as said below
- pattern: int32 [448, 448], P('row', 'col'), may hold values 0 or 1
Outputs:
- sign_matrix: float32 [5824, 5824], P('row', 'col')
Inputs may be any that keep to these rules, and one draw needn't show every extreme that they name: `new_atom`: each old atom appears once. Block column b holds atoms b * 28 to (b + 1) * 28 - 1 in both orders. For each new block column d and each v from 0 to 27, exactly one atom of new block column d comes from old block column (d - 1 - (v mod 16)) mod 16, so the number of atoms that old block column b sends to new block column (b + k) mod 16 is the number of such v with (1 + v) mod 16 = k.
All inputs are finite; a program needn't handle non-finite values. No bound on the sum of `pattern` on one device may be relied on, other than what follows from the above.
Results may differ from a plain program's by a relative error of at most 0.0029.
Values may be sent and summed in bfloat16 or wider, within the bound.
No kernel may reach another device: no remote copies, remote signals or barrier semaphores. Data moves between devices by JAX's collectives and lax.ppermute only.
A program may use at most 64 MiB of HBM per device.

v0:
```python
import functools
import jax
import jax.numpy as jnp
import numpy as np
from jax import lax
from jax.sharding import Mesh
from jax.sharding import PartitionSpec as P

NBF = 13
ROW = ("row_0", "row_1")
COL = ("col_0", "col_1")
ROW_COL = ("row_0", "row_1", "col_0", "col_1")


def by_axis(array, axes):
    return functools.reduce(lax.psum, axes, array)


def expand(atoms):
    return (atoms[:, None] * NBF + jnp.arange(NBF, dtype=jnp.int32)[None, :]).reshape(-1)


def pack_slots(new_atom, here, per_block, groups, slots):
    source = new_atom.reshape(groups, per_block) // per_block
    local = new_atom.reshape(groups, per_block) - here * per_block
    mine = source == here
    rank = jnp.cumsum(mine.astype(jnp.int32), axis=1) - 1
    number = jnp.arange(slots, dtype=jnp.int32)
    hit = mine[:, None, :] & (rank[:, None, :] == number[None, :, None])
    atoms = jnp.sum(jnp.where(hit, local[:, None, :], 0), axis=2)
    used = jnp.any(hit, axis=2)
    return (atoms.reshape(-1), jnp.repeat(used.reshape(-1), NBF))


def place_slots(new_atom, here, per_block, groups, slots):
    source = lax.dynamic_slice_in_dim(new_atom, here * per_block, per_block) // per_block
    onehot = source[:, None] == jnp.arange(groups, dtype=jnp.int32)[None, :]
    running = jnp.cumsum(onehot.astype(jnp.int32), axis=0) - 1
    rank = jnp.sum(jnp.where(onehot, running, 0), axis=1)
    return expand((source * slots + rank).astype(jnp.int32))


def fold_right(row_panel, right):
    return jnp.dot(
        row_panel,
        lax.all_gather(right, ROW, axis=0, tiled=True),
        preferred_element_type=jnp.float32,
    )


def on_device(hamiltonian, new_atom, pattern):
    rows_here, cols_here = hamiltonian.shape
    row_count = lax.axis_size(ROW)
    col_count = lax.axis_size(COL)
    order_all = rows_here * row_count
    atoms_row = rows_here // NBF
    atoms_col = cols_here // NBF
    ratio = col_count // row_count
    counts = np.bincount((1 + np.arange(atoms_col)) % col_count, minlength=col_count)
    targets = (np.arange(ratio)[:, None] + np.arange(col_count)[None, :]) % col_count // ratio
    per_target = np.sum(
        (targets[None, :, :] == np.arange(row_count)[:, None, None]) * counts[None, None, :],
        axis=(1, 2),
    )
    slots_row = max(int(np.max(per_target)), 1)
    slots_col = max(int(np.max(counts)), 1)
    row_here = lax.axis_index(ROW)
    col_here = lax.axis_index(COL)
    atoms, flags = pack_slots(new_atom, row_here, atoms_row, row_count, slots_row)
    outgoing = jnp.where(
        flags[:, None], jnp.take(hamiltonian, expand(atoms), axis=0), jnp.zeros((), jnp.bfloat16)
    )
    arrived = lax.all_to_all(outgoing, ROW, split_axis=0, concat_axis=0, tiled=True)
    moved = jnp.take(
        arrived, place_slots(new_atom, row_here, atoms_row, row_count, slots_row), axis=0
    )
    atoms, flags = pack_slots(new_atom, col_here, atoms_col, col_count, slots_col)
    outgoing = jnp.where(
        flags[None, :], jnp.take(moved, expand(atoms), axis=1), jnp.zeros((), jnp.bfloat16)
    )
    arrived = lax.all_to_all(outgoing, COL, split_axis=1, concat_axis=1, tiled=True)
    moved = jnp.take(
        arrived, place_slots(new_atom, col_here, atoms_col, col_count, slots_col), axis=1
    )
    atom_rows, atom_cols = pattern.shape
    keep = jnp.broadcast_to(
        pattern.astype(jnp.float32)[:, None, :, None], (atom_rows, NBF, atom_cols, NBF)
    ).reshape(rows_here, cols_here)
    masked = moved.astype(jnp.float32) * keep
    total = by_axis(jnp.sum(masked * masked), ROW_COL)
    start = (masked * lax.rsqrt(total / order_all)).astype(jnp.bfloat16)
    kept = lax.all_gather(start, COL, axis=1, tiled=True)
    square = (fold_right(kept, start) * keep).astype(jnp.bfloat16)
    cube = fold_right(kept, square) * keep
    return keep * (1.5 * start.astype(jnp.float32) - 0.5 * cube)


def solution(mesh):
    split = Mesh(mesh.devices.reshape(4, 2, 4, 4), ("row_0", "row_1", "col_0", "col_1"))
    in_specs = (P(ROW, COL), P(), P(ROW, COL))
    out_specs = P(ROW, COL)
    return jax.shard_map(
        on_device, mesh=split, in_specs=in_specs, out_specs=out_specs, check_vma=False
    )
```

profile of v0, /device:TPU:1, one launch (start us, length us, event | category | flops | bytes accessed | tf_op | source)
XLA Modules:
  0.0 264.0 jit_solution(595021071242153486)
XLA Ops:
  6.5 0.8 fusion.18
  7.4 0.7 broadcast_divide_fusion.1
  8.3 0.2 reduce_window_sum.47
  8.5 0.2 fusion.9
  8.7 0.2 select_reduce_fusion
  9.4 0.2 add.321
  9.7 3.5 %gather_fusion = bf16[832,364]{1,0:T(8,128)(2,1)S(1)} fusion(bf16[728,364]{1,0:T(8,128)(2,1)S(1)} %copy-done, s32[1024]{0:T(1024)S(1)} %pad_clamp_fusion.3), kind=kCustom, calls=%fused_computation | custom fusion | bytes 1214720 | tf_op jit(solution)/shard_map/jit(_take)/gather | solution.py:71
  13.2 1.1 select_select_fusion.1
  14.4 5.8 %all-to-all-start = ((bf16[8,104,364]{2,1,0:T(8,128)(2,1)}), bf16[8,104,364]{2,1,0:T(8,128)(2,1)S(1)}, u32[]{:S(2)}, u32[]{:S(2)}) async-start(bf16[8,104,364]{2,1,0:T(8,128)(2,1)} %select_select_fusion.1), calls=%async_computation | async-start | bytes 1277952 | tf_op jit(solution)/shard_map/all_to_all | solution.py:73
  20.4 0.2 select_reduce_fusion.1
  20.8 0.1 add.324
  20.9 0.1 add.308
  21.3 0.2 reduce_window_sum.45
  21.5 0.1 fusion.13
  21.9 0.1 select_reduce_fusion.2
  22.4 0.1 add.330
  22.7 0.2 select_reduce_fusion.3
  23.1 7.8 %all-to-all-done = bf16[8,104,364]{2,1,0:T(8,128)(2,1)S(1)} async-done(((bf16[8,104,364]{2,1,0:T(8,128)(2,1)}), bf16[8,104,364]{2,1,0:T(8,128)(2,1)S(1)}, u32[]{:S(2)}, u32[]{:S(2)}) %all-to-all-start) | async-done | bytes 605728 | tf_op jit(solution)/shard_map/all_to_all | solution.py:73
  30.9 3.0 %gather_fusion.1 = bf16[728,364]{1,0:T(8,128)(2,1)S(1)} fusion(bf16[832,364]{1,0:T(8,128)(2,1)S(1)} %bitcast.35, s32[1024]{0:T(1024)S(1)} %pad_clamp_fusion.2), kind=kCustom, calls=%fused_computation.1 | custom fusion | bytes 1062880 | tf_op jit(solution)/shard_map/jit(_take)/gather | solution.py:74
  33.8 0.2 broadcast_select_fusion
  34.0 0.2 copy.30
  34.3 2.2 gather_fusion.2
  36.4 0.2 gather.24
  36.7 1.1 select_select_fusion
  37.8 7.9 %all-to-all-start.1 = ((bf16[728,16,26]{0,2,1:T(8,128)(2,1)}), bf16[728,16,26]{0,2,1:T(8,128)(2,1)}, u32[]{:S(2)}, u32[]{:S(2)}) async-start(bf16[728,16,26]{0,2,1:T(8,128)(2,1)} %select_select_fusion), calls=%async_computation.1 | async-start | bytes 1572864 | tf_op jit(solution)/shard_map/all_to_all | solution.py:81
  45.8 0.1 broadcast_in_dim.154
  46.2 4.7 %broadcast_in_dim.132 = f32[56,13,28,13]{1,0,3,2:T(8,128)} broadcast(f32[56,28]{0,1:T(8,128)S(1)} %convert_element_type.41), dimensions={0,2} | broadcast | bytes 1066240 | tf_op jit(solution)/shard_map/broadcast_in_dim | solution.py:86
  50.9 6.7 %reshape.368 = f32[728,364]{0,1:T(8,128)S(1)} reshape(f32[56,13,28,13]{1,0,3,2:T(8,128)} %broadcast_in_dim.132) | data formatting | bytes 2119936 | tf_op jit(solution)/shard_map/reshape | solution.py:88
  57.6 0.4 copy.38
  58.0 0.5 all-to-all-done.1
  58.5 1.5 all_to_all.15
  60.0 2.2 gather_fusion.3
  62.1 0.3 copy.31
  62.4 0.9 fusion.5
  63.3 7.5 %psum.28 = f32[]{:T(128)} all-reduce(f32[]{:T(128)} %fusion.5), channel_id=1, replica_groups=mesh['row_0'=4,'row_1'=2,'col_0'=4,'col_1'=4] {'row_0'}, use_global_device_ids=true, to_apply=%region_11.12 | all-reduce | flops 1 | bytes 8 | tf_op jit(solution)/shard_map/psum | solution.py:16
  70.8 7.3 %psum.29 = f32[]{:T(128)} all-reduce(f32[]{:T(128)} %psum.28), channel_id=1, replica_groups=mesh['row_0'=4,'row_1'=2,'col_0'=4,'col_1'=4] {'row_1'}, use_global_device_ids=true, to_apply=%region_12.13 | all-reduce | flops 1 | bytes 8 | tf_op jit(solution)/shard_map/psum | solution.py:16
  78.2 7.6 %psum.30 = f32[]{:T(128)} all-reduce(f32[]{:T(128)} %psum.29), channel_id=1, replica_groups=mesh['row_0'=4,'row_1'=2,'col_0'=4,'col_1'=4] {'col_0'}, use_global_device_ids=true, to_apply=%region_13.14 | all-reduce | flops 1 | bytes 8 | tf_op jit(solution)/shard_map/psum | solution.py:16
  85.8 9.0 %psum.31 = f32[]{:T(128)} all-reduce(f32[]{:T(128)} %psum.30), channel_id=1, replica_groups=mesh['row_0'=4,'row_1'=2,'col_0'=4,'col_1'=4] {'col_1'}, use_global_device_ids=true, to_apply=%region_14.15 | all-reduce | flops 1 | bytes 8 | tf_op jit(solution)/shard_map/psum | solution.py:16
  95.5 1.0 fusion.7
  96.6 0.7 all-gather.5.cloned.1.call-update
  97.3 0.2 all-gather.7.cloned.1.call-start
  97.5 71.0 %all-gather.9.cloned.1.call-done = bf16[16,364,728]{1,2,0:T(8,128)(2,1)} async-done(((bf16[1,364,728]{1,2,0:T(8,128)(2,1)}), bf16[16,364,728]{1,2,0:T(8,128)(2,1)}) %all-gather.9.cloned.1.call-update) | async-done | bytes 8479760 | tf_op jit(solution)/shard_map/all_gather | solution.py:92
  168.5 8.1 %copy.35 = bf16[16,364,728]{1,0,2:T(8,128)(2,1)} copy(bf16[16,364,728]{1,2,0:T(8,128)(2,1)} %all-gather.9.cloned.1.call-done) | data formatting | bytes 16959488 | tf_op jit(solution)/shard_map/all_gather | solution.py:92
  176.7 15.8 %reshape.402 = bf16[5824,728]{0,1:T(8,128)(2,1)} reshape(bf16[16,364,728]{1,0,2:T(8,128)(2,1)} %copy.35) | data formatting | bytes 16959488
  192.5 11.0 %all-gather.5.cloned.1.call-done = bf16[5824,364]{1,0:T(8,128)(2,1)} async-done(((bf16[728,364]{1,0:T(8,128)(2,1)}), bf16[5824,364]{1,0:T(8,128)(2,1)}) %all-gather.5.cloned.1.call-update) | async-done | bytes 4239888 | tf_op jit(solution)/shard_map/all_gather | solution.py:46
  203.5 10.2 %fusion.3 = bf16[728,364]{1,0:T(8,128)(2,1)} fusion(f32[728,364]{1,0:T(8,128)S(1)} %copy.38, bf16[5824,728]{0,1:T(8,128)(2,1)} %reshape.402, bf16[5824,364]{1,0:T(8,128)(2,1)} %all-gather.5.cloned.1.call-done), kind=kOutput, calls=%fused_computation.9 | convolution fusion | flops 3087156736 | bytes 14309568 | tf_op jit(solution)/shard_map/dot_general | solution.py:44
  213.7 33.4 %all-gather.7.cloned.1.call-done = bf16[5824,364]{1,0:T(8,128)(2,1)} async-done(((bf16[728,364]{1,0:T(8,128)(2,1)}), bf16[5824,364]{1,0:T(8,128)(2,1)}) %all-gather.7.cloned.1.call-update) | async-done | bytes 4239888 | tf_op jit(solution)/shard_map/all_gather | solution.py:46
  247.1 10.3 %fusion.2 = f32[728,364]{1,0:T(8,128)} fusion(f32[728,364]{1,0:T(8,128)S(1)} %copy.38, bf16[5824,728]{0,1:T(8,128)(2,1)} %reshape.402, bf16[5824,364]{1,0:T(8,128)(2,1)} %all-gather.7.cloned.1.call-done, bf16[728,364]{1,0:T(8,128)(2,1)S(1)} %copy-done.1), kind=kOutput, calls=%fused_computation.8 | convolution fusion | flops 3088216576 | bytes 15369536 | tf_op jit(solution)/shard_map/dot_general | solution.py:44
  (68 shorter events, 3.0 us)
Async XLA Ops:
  6.5 3.2 %copy-start = (bf16[728,364]{1,0:T(8,128)(2,1)S(1)}, bf16[728,364]{1,0:T(8,128)(2,1)}, u32[]{:S(2)}) copy-start(bf16[728,364]{1,0:T(8,128)(2,1)} %param.3) | copy-start | bytes 1589956
  13.2 6.9 %copy-start.3 = (s32[448]{0:T(512)S(1)}, s32[448]{0:T(512)}, u32[]{:S(2)}) copy-start(s32[448]{0:T(512)} %param.4) | copy-start | bytes 5380
  14.4 16.5 %all-to-all-start = ((bf16[8,104,364]{2,1,0:T(8,128)(2,1)}), bf16[8,104,364]{2,1,0:T(8,128)(2,1)S(1)}, u32[]{:S(2)}, u32[]{:S(2)}) async-start(bf16[8,104,364]{2,1,0:T(8,128)(2,1)} %select_select_fusion.1), calls=%async_computation | async-start | bytes 1277952 | tf_op jit(solution)/shard_map/all_to_all | solution.py:73
  37.8 8.4 %copy-start.2 = (s32[56,28]{0,1:T(8,128)S(1)}, s32[56,28]{0,1:T(8,128)}, u32[]{:S(2)}) copy-start(s32[56,28]{0,1:T(8,128)} %param.5) | copy-start | bytes 18820
  37.8 20.8 %all-to-all-start.1 = ((bf16[728,16,26]{0,2,1:T(8,128)(2,1)}), bf16[728,16,26]{0,2,1:T(8,128)(2,1)}, u32[]{:S(2)}, u32[]{:S(2)}) async-start(bf16[728,16,26]{0,2,1:T(8,128)(2,1)} %select_select_fusion), calls=%async_computation.1 | async-start | bytes 1572864 | tf_op jit(solution)/shard_map/all_to_all | solution.py:81
  45.7 122.8 %all-gather.9.cloned.1.call-start = ((), (), s32[]{:S(2)}) async-start(), calls=%async_computation.4 | async-start | bytes 9504768 | tf_op jit(solution)/shard_map/all_gather | solution.py:92
  96.5 107.0 %all-gather.5.cloned.1.call-start = ((), (), s32[]{:S(2)}) async-start(), calls=%async_computation.2 | async-start | bytes 5031936 | tf_op jit(solution)/shard_map/all_gather | solution.py:46
  97.3 149.8 %all-gather.7.cloned.1.call-start = ((), (), s32[]{:S(2)}) async-start(), calls=%async_computation.3 | async-start | bytes 5031936 | tf_op jit(solution)/shard_map/all_gather | solution.py:46
  192.5 54.6 %copy-start.1 = (bf16[728,364]{1,0:T(8,128)(2,1)S(1)}, bf16[728,364]{1,0:T(8,128)(2,1)}, u32[]{:S(2)}) copy-start(bf16[728,364]{1,0:T(8,128)(2,1)} %fusion.7) | copy-start | bytes 1589956
Sparse Core Ops, SparseCore 0:
  96.7 71.8 all-gather.8
  170.2 33.2 all-gather.4
  213.8 33.2 all-gather.6
where the time goes:
time: 265 us; the launch traced here: 264 us
  waiting for transfers between devices  124 us (47%)
  local copies, waits for them, and re-layouts  51.2 us (19%)
  blocking collectives  31.4 us (12%)
  matrix products  20.5 us (8%)
  between operations  14.1 us (5%)
  starting transfers between devices  14 us (5%)
  other arithmetic  8.34 us (3%)
    all_gather x1, waiting for transfers between devices, on_device(): kept = lax.all_gather(start, COL, axis=1, tiled=True)  71 us
    all_gather x2, waiting for transfers between devices, fold_right(): lax.all_gather(right, ROW, axis=0, tiled=True)  44.4 us
    psum x4, blocking collectives, by_axis(): return functools.reduce(lax.psum, axes, array)  31.4 us
    dot_general x2, matrix products, fold_right(): jnp.dot(row_panel, lax.all_gather(right, ROW, axis=0, tiled=True), prefer...  20.5 us
    unnamed x9, local copies, waits for them, and re-layouts  15.9 us
    all_gather x1, local copies, waits for them, and re-layouts, on_device(): kept = lax.all_gather(start, COL, axis=1, tiled=True)  8.14 us
    all_to_all x1, starting transfers between devices, on_device(): lax.all_to_all(outgoing, COL, split_axis=1, concat_axis=1, tiled=True)  7.94 us
    all_to_all x1, waiting for transfers between devices, on_device(): lax.all_to_all(outgoing, ROW, split_axis=0, concat_axis=0, tiled=True)  7.77 us
  transfers between devices with their start and end apart: 5, of which 5 were waited for; matrix products, arithmetic and copies ran while one was open for 15% of the time, Pallas kernels for 0%

commit v1 on v0

--- a/solution.py
+++ b/solution.py
@@ -89,7 +89,9 @@
     masked = moved.astype(jnp.float32) * keep
     total = by_axis(jnp.sum(masked * masked), ROW_COL)
     start = (masked * lax.rsqrt(total / order_all)).astype(jnp.bfloat16)
-    kept = lax.all_gather(start, COL, axis=1, tiled=True)
+    kept = jnp.concatenate(
+        lax.all_to_all(jnp.stack([start] * lax.axis_size(COL)), COL, 0, 0), axis=1
+    )
     square = (fold_right(kept, start) * keep).astype(jnp.bfloat16)
     cube = fold_right(kept, square) * keep
     return keep * (1.5 * start.astype(jnp.float32) - 0.5 * cube)

time: 265 us -> 318 us (1.20)
  waiting for transfers between devices: 124 us -> 169 us
  starting transfers between devices: 14 us -> 18.8 us
  local copies, waits for them, and re-layouts: 51.2 us -> 55.2 us
    all_to_all x0 -> x1, waiting for transfers between devices: none -> 118 us  [on_device(): lax.all_to_all(jnp.stack([start] * lax.axis_size(COL)), COL, 0, 0)]
    all_gather x1 -> x0, waiting for transfers between devices: 71 us -> none  [on_device(): kept = lax.all_gather(start, COL, axis=1, tiled=True)]
    reshape x0 -> x2, local copies, waits for them, and re-layouts: none -> 23.8 us  [on_device(): jnp.concatenate(lax.all_to_all(jnp.stack([start] * lax.axis_size(COL)), C...]
    unnamed x9 -> x12, local copies, waits for them, and re-layouts: 15.9 us -> 0.03 us
    all_gather x1 -> x0, local copies, waits for them, and re-layouts: 8.14 us -> none  [on_device(): kept = lax.all_gather(start, COL, axis=1, tiled=True)]
    all_to_all x0 -> x1, starting transfers between devices: none -> 4.75 us  [on_device(): lax.all_to_all(jnp.stack([start] * lax.axis_size(COL)), COL, 0, 0)]
    another operation x0 -> x1, local copies, waits for them, and re-layouts: none -> 4.22 us  [on_device(): jnp.stack([start] * lax.axis_size(COL))]
    all_gather x2, waiting for transfers between devices: 44.4 us -> 41.2 us  [fold_right(): lax.all_gather(right, ROW, axis=0, tiled=True)]
  transfers between devices with their start and end apart: 5 -> 5, of which waited for: 5 -> 4; matrix products, arithmetic and copies ran while one was open for 15% -> 12% of each run, Pallas kernels for 0% -> 0%
where the time goes in v1:
time: 318 us; the launch traced here: 317 us
  waiting for transfers between devices  169 us (53%)
  local copies, waits for them, and re-layouts  55.2 us (17%)
  blocking collectives  31.3 us (10%)
  matrix products  20.6 us (6%)
  starting transfers between devices  18.8 us (6%)
  between operations  14.5 us (5%)
  other arithmetic  7.54 us (2%)
    all_to_all x1, waiting for transfers between devices, on_device(): lax.all_to_all(jnp.stack([start] * lax.axis_size(COL)), COL, 0, 0)  118 us
    all_gather x2, waiting for transfers between devices, fold_right(): lax.all_gather(right, ROW, axis=0, tiled=True)  41.2 us
    psum x4, blocking collectives, by_axis(): return functools.reduce(lax.psum, axes, array)  31.3 us
    reshape x2, local copies, waits for them, and re-layouts, on_device(): jnp.concatenate(lax.all_to_all(jnp.stack([start] * lax.axis_size(COL)), C...  23.8 us
    dot_general x2, matrix products, fold_right(): jnp.dot(row_panel, lax.all_gather(right, ROW, axis=0, tiled=True), prefer...  20.6 us
    all_to_all x1, starting transfers between devices, on_device(): lax.all_to_all(outgoing, COL, split_axis=1, concat_axis=1, tiled=True)  7.94 us
    all_to_all x1, waiting for transfers between devices, on_device(): lax.all_to_all(outgoing, ROW, split_axis=0, concat_axis=0, tiled=True)  7.78 us
    reshape x2, local copies, waits for them, and re-layouts, on_device(): keep = jnp.broadcast_to(pattern.astype(jnp.float32)[:, None, :, None], (a...  7.1 us
  transfers between devices with their start and end apart: 5, of which 4 were waited for; matrix products, arithmetic and copies ran while one was open for 12% of the time, Pallas kernels for 0%

profile of v1, /device:TPU:1, one launch (start us, length us, event | category | flops | bytes accessed | tf_op | source)
XLA Modules:
  0.0 316.5 jit_solution(13466056134711212944)
XLA Ops:
  6.5 0.8 fusion.18
  7.3 0.7 broadcast_divide_fusion.1
  8.2 0.2 reduce_window_sum.47
  8.5 0.2 fusion.9
  8.7 0.2 select_reduce_fusion
  9.1 0.2 add.321
  9.7 3.5 %gather_fusion = bf16[832,364]{1,0:T(8,128)(2,1)S(1)} fusion(bf16[728,364]{1,0:T(8,128)(2,1)S(1)} %copy-done, s32[1024]{0:T(1024)S(1)} %pad_clamp_fusion.3), kind=kCustom, calls=%fused_computation | custom fusion | bytes 1214720 | tf_op jit(solution)/shard_map/jit(_take)/gather | solution.py:71
  13.2 1.1 select_select_fusion.1
  14.4 5.8 %all-to-all-start = ((bf16[8,104,364]{2,1,0:T(8,128)(2,1)}), bf16[8,104,364]{2,1,0:T(8,128)(2,1)S(1)}, u32[]{:S(2)}, u32[]{:S(2)}) async-start(bf16[8,104,364]{2,1,0:T(8,128)(2,1)} %select_select_fusion.1), calls=%async_computation | async-start | bytes 1277952 | tf_op jit(solution)/shard_map/all_to_all | solution.py:73
  20.4 0.2 select_reduce_fusion.1
  20.8 0.1 add.324
  20.9 0.1 add.308
  21.3 0.2 reduce_window_sum.45
  21.6 0.1 fusion.13
  21.7 0.1 select_reduce_fusion.2
  22.1 0.1 add.330
  22.8 0.2 select_reduce_fusion.3
  23.1 7.8 %all-to-all-done = bf16[8,104,364]{2,1,0:T(8,128)(2,1)S(1)} async-done(((bf16[8,104,364]{2,1,0:T(8,128)(2,1)}), bf16[8,104,364]{2,1,0:T(8,128)(2,1)S(1)}, u32[]{:S(2)}, u32[]{:S(2)}) %all-to-all-start) | async-done | bytes 605728 | tf_op jit(solution)/shard_map/all_to_all | solution.py:73
  30.9 3.0 gather_fusion.1
  33.8 0.2 broadcast_select_fusion
  34.0 0.2 copy.29
  34.3 2.2 gather_fusion.2
  36.5 0.2 gather.24
  36.7 1.1 select_select_fusion
  37.8 7.9 %all-to-all-start.1 = ((bf16[728,16,26]{0,2,1:T(8,128)(2,1)}), bf16[728,16,26]{0,2,1:T(8,128)(2,1)}, u32[]{:S(2)}, u32[]{:S(2)}) async-start(bf16[728,16,26]{0,2,1:T(8,128)(2,1)} %select_select_fusion), calls=%async_computation.1 | async-start | bytes 1572864 | tf_op jit(solution)/shard_map/all_to_all | solution.py:81
  46.1 4.7 %broadcast_in_dim.132 = f32[56,13,28,13]{1,0,3,2:T(8,128)} broadcast(f32[56,28]{0,1:T(8,128)S(1)} %convert_element_type.45), dimensions={0,2} | broadcast | bytes 1066240 | tf_op jit(solution)/shard_map/broadcast_in_dim | solution.py:86
  50.8 6.7 %reshape.386 = f32[728,364]{0,1:T(8,128)S(1)} reshape(f32[56,13,28,13]{1,0,3,2:T(8,128)} %broadcast_in_dim.132) | data formatting | bytes 2119936 | tf_op jit(solution)/shard_map/reshape | solution.py:88
  57.6 0.4 copy.37
  58.0 0.6 all-to-all-done.1
  58.5 1.5 all_to_all.18
  60.0 2.2 gather_fusion.3
  62.1 0.3 copy.30
  62.4 0.9 fusion.5
  63.4 7.5 %psum.28 = f32[]{:T(128)} all-reduce(f32[]{:T(128)} %fusion.5), channel_id=1, replica_groups=mesh['row_0'=4,'row_1'=2,'col_0'=4,'col_1'=4] {'row_0'}, use_global_device_ids=true, to_apply=%region_11.12 | all-reduce | flops 1 | bytes 8 | tf_op jit(solution)/shard_map/psum | solution.py:16
  70.8 7.3 %psum.29 = f32[]{:T(128)} all-reduce(f32[]{:T(128)} %psum.28), channel_id=1, replica_groups=mesh['row_0'=4,'row_1'=2,'col_0'=4,'col_1'=4] {'row_1'}, use_global_device_ids=true, to_apply=%region_12.13 | all-reduce | flops 1 | bytes 8 | tf_op jit(solution)/shard_map/psum | solution.py:16
  78.2 7.6 %psum.30 = f32[]{:T(128)} all-reduce(f32[]{:T(128)} %psum.29), channel_id=1, replica_groups=mesh['row_0'=4,'row_1'=2,'col_0'=4,'col_1'=4] {'col_0'}, use_global_device_ids=true, to_apply=%region_13.14 | all-reduce | flops 1 | bytes 8 | tf_op jit(solution)/shard_map/psum | solution.py:16
  85.8 9.0 %psum.31 = f32[]{:T(128)} all-reduce(f32[]{:T(128)} %psum.30), channel_id=1, replica_groups=mesh['row_0'=4,'row_1'=2,'col_0'=4,'col_1'=4] {'col_1'}, use_global_device_ids=true, to_apply=%region_14.15 | all-reduce | flops 1 | bytes 8 | tf_op jit(solution)/shard_map/psum | solution.py:16
  95.5 0.2 fusion.7
  95.7 4.2 %stack.2 = bf16[16,728,364]{2,1,0:T(8,128)(2,1)} broadcast(bf16[728,364]{1,0:T(8,128)(2,1)S(1)} %fusion.7), dimensions={1,2} | broadcast | bytes 9009728 | tf_op jit(solution)/shard_map/stack | solution.py:93
  99.9 4.7 %all-to-all-start.2 = ((bf16[16,728,364]{2,1,0:T(8,128)(2,1)}), bf16[16,728,364]{2,1,0:T(8,128)(2,1)}, u32[]{:S(2)}, u32[]{:S(2)}) async-start(bf16[16,728,364]{2,1,0:T(8,128)(2,1)} %stack.2), calls=%async_computation.2 | async-start | bytes 17891328 | tf_op jit(solution)/shard_map/all_to_all | solution.py:93
  104.7 0.7 all-gather.3.cloned.1.call-update
  105.4 0.2 all-gather.5.cloned.1.call-start
  105.6 118.4 %all-to-all-done.2 = bf16[16,728,364]{2,1,0:T(8,128)(2,1)} async-done(((bf16[16,728,364]{2,1,0:T(8,128)(2,1)}), bf16[16,728,364]{2,1,0:T(8,128)(2,1)}, u32[]{:S(2)}, u32[]{:S(2)}) %all-to-all-start.2) | async-done | bytes 8479776 | tf_op jit(solution)/shard_map/all_to_all | solution.py:93
  224.0 8.1 %copy.34 = bf16[728,16,364]{2,1,0:T(8,128)(2,1)} copy(bf16[728,16,364]{2,0,1:T(8,128)(2,1)} %bitcast.6) | data formatting | bytes 16959488 | tf_op jit(solution)/shard_map/reshape | solution.py:92
  232.2 15.7 %reshape.388 = bf16[728,5824]{1,0:T(8,128)(2,1)} reshape(bf16[728,16,364]{2,1,0:T(8,128)(2,1)} %copy.34) | data formatting | bytes 16959488 | tf_op jit(solution)/shard_map/reshape | solution.py:92
  247.9 10.2 %fusion.3 = bf16[728,364]{1,0:T(8,128)(2,1)} fusion(f32[728,364]{1,0:T(8,128)S(1)} %copy.37, bf16[728,5824]{1,0:T(8,128)(2,1)} %reshape.388, bf16[5824,364]{1,0:T(8,128)(2,1)} %all-gather.3.cloned.1.call-done), kind=kOutput, calls=%fused_computation.9 | convolution fusion | flops 3087156736 | bytes 14309568 | tf_op jit(solution)/shard_map/dot_general | solution.py:44
  258.1 41.2 %all-gather.5.cloned.1.call-done = bf16[5824,364]{1,0:T(8,128)(2,1)} async-done(((bf16[728,364]{1,0:T(8,128)(2,1)}), bf16[5824,364]{1,0:T(8,128)(2,1)}) %all-gather.5.cloned.1.call-update) | async-done | bytes 4239888 | tf_op jit(solution)/shard_map/all_gather | solution.py:46
  299.3 10.4 %fusion.2 = f32[728,364]{1,0:T(8,128)} fusion(f32[728,364]{1,0:T(8,128)S(1)} %copy.37, bf16[728,5824]{1,0:T(8,128)(2,1)} %reshape.388, bf16[5824,364]{1,0:T(8,128)(2,1)} %all-gather.5.cloned.1.call-done, bf16[728,364]{1,0:T(8,128)(2,1)S(1)} %copy-done.3), kind=kOutput, calls=%fused_computation.8 | convolution fusion | flops 3088216576 | bytes 15369536 | tf_op jit(solution)/shard_map/dot_general | solution.py:44
  (72 shorter events, 3.1 us)
Async XLA Ops:
  6.5 3.2 %copy-start = (bf16[728,364]{1,0:T(8,128)(2,1)S(1)}, bf16[728,364]{1,0:T(8,128)(2,1)}, u32[]{:S(2)}) copy-start(bf16[728,364]{1,0:T(8,128)(2,1)} %param.3) | copy-start | bytes 1589956
  13.2 6.9 %copy-start.5 = (s32[448]{0:T(512)S(1)}, s32[448]{0:T(512)}, u32[]{:S(2)}) copy-start(s32[448]{0:T(512)} %param.4) | copy-start | bytes 5380
  14.4 16.5 %all-to-all-start = ((bf16[8,104,364]{2,1,0:T(8,128)(2,1)}), bf16[8,104,364]{2,1,0:T(8,128)(2,1)S(1)}, u32[]{:S(2)}, u32[]{:S(2)}) async-start(bf16[8,104,364]{2,1,0:T(8,128)(2,1)} %select_select_fusion.1), calls=%async_computation | async-start | bytes 1277952 | tf_op jit(solution)/shard_map/all_to_all | solution.py:73
  37.8 8.3 %copy-start.4 = (s32[56,28]{0,1:T(8,128)S(1)}, s32[56,28]{0,1:T(8,128)}, u32[]{:S(2)}) copy-start(s32[56,28]{0,1:T(8,128)} %param.5) | copy-start | bytes 18820
  37.8 20.8 %all-to-all-start.1 = ((bf16[728,16,26]{0,2,1:T(8,128)(2,1)}), bf16[728,16,26]{0,2,1:T(8,128)(2,1)}, u32[]{:S(2)}, u32[]{:S(2)}) async-start(bf16[728,16,26]{0,2,1:T(8,128)(2,1)} %select_select_fusion), calls=%async_computation.1 | async-start | bytes 1572864 | tf_op jit(solution)/shard_map/all_to_all | solution.py:81
  95.7 4.2 %copy-start.2 = (bf16[728,364]{1,0:T(8,128)(2,1)}, bf16[728,364]{1,0:T(8,128)(2,1)S(1)}, u32[]{:S(2)}) copy-start(bf16[728,364]{1,0:T(8,128)(2,1)S(1)} %fusion.7) | copy-start | bytes 1589956
  99.9 124.1 %all-to-all-start.2 = ((bf16[16,728,364]{2,1,0:T(8,128)(2,1)}), bf16[16,728,364]{2,1,0:T(8,128)(2,1)}, u32[]{:S(2)}, u32[]{:S(2)}) async-start(bf16[16,728,364]{2,1,0:T(8,128)(2,1)} %stack.2), calls=%async_computation.2 | async-start | bytes 17891328 | tf_op jit(solution)/shard_map/all_to_all | solution.py:93
  104.7 143.2 %all-gather.3.cloned.1.call-start = ((), (), s32[]{:S(2)}) async-start(), calls=%async_computation.3 | async-start | bytes 5031936 | tf_op jit(solution)/shard_map/all_gather | solution.py:46
  105.4 193.9 %all-gather.5.cloned.1.call-start = ((), (), s32[]{:S(2)}) async-start(), calls=%async_computation.4 | async-start | bytes 5031936 | tf_op jit(solution)/shard_map/all_gather | solution.py:46
  247.9 51.4 %copy-start.3 = (bf16[728,364]{1,0:T(8,128)(2,1)S(1)}, bf16[728,364]{1,0:T(8,128)(2,1)}, u32[]{:S(2)}) copy-start(bf16[728,364]{1,0:T(8,128)(2,1)} %copy-done.2) | copy-start | bytes 1589956
  299.3 10.4 %copy-start.1 = (bf16[728,364]{1,0:T(8,128)(2,1)S(1)}, bf16[728,364]{1,0:T(8,128)(2,1)}, u32[]{:S(2)}) copy-start(bf16[728,364]{1,0:T(8,128)(2,1)} %param.3) | copy-start | bytes 1589956
Sparse Core Ops, SparseCore 0:
  107.2 36.6 all-gather.2
  258.3 40.9 all-gather.4
